TPU v7x, 32 devices: a whole 2x2x4 slice. The times are simulated.
32 devices in a mesh: win: 8 (over z, y), var: 4 (over x, core).
Axes of the slice: x: 2, y: 2, z: 4, core: 2. Of those that a mesh axis runs over, the one named last changes fastest.
Arguments:
- inputs: bfloat16 [96, 256, 512], P('win', 'var'), may hold values from -6 to 6
- counts: int32 [96], P('win'), may hold values from 8 to 256, as said below
- row_index: int32 [96, 256], P('win'), may hold values from 0 to 255, each once within a row
- w_qkv: bfloat16 [2, 512, 1536], replicated, may hold values from -0.25 to 0.25
- bias_qv: float32 [2, 1024], replicated, may hold values from -2 to 2
- w_attn_out: bfloat16 [2, 512, 512], replicated, may hold values from -0.75 to 0.75
- out_bias: float32 [2, 2, 512], replicated, may hold values from -2 to 2
- w_in: bfloat16 [2, 512, 2048], replicated, may hold values from -0.25 to 0.25
- bias_in: float32 [2, 2048], replicated, may hold values from -2 to 2
- w_ffn_out: bfloat16 [2, 2048, 512], replicated, may hold values from -0.125 to 0.125
- norm_gain: float32 [2, 2, 512], replicated, may hold values from 0.5 to 1.5
- norm_bias: float32 [2, 2, 512], replicated, may hold values from -2 to 2
- cotangent: bfloat16 [96, 256, 512], P('win', 'var'), may hold values from -6 to 6
Outputs:
- layer_out: bfloat16 [96, 256, 512], P('win', 'var')
- grad_inputs: float32 [96, 256, 512], P('win', 'var')
- grad_qkv: float32 [2, 512, 1536], P(None, 'var')
- grad_bias_qv: float32 [2, 1024], P(None, 'var')
- grad_attn_out: float32 [2, 512, 512], P(None, 'var')
- grad_out_bias: float32 [2, 2, 512], P(None, None, 'var')
- grad_in: float32 [2, 512, 2048], P(None, 'var')
- grad_bias_in: float32 [2, 2048], P(None, 'var')
- grad_ffn_out: float32 [2, 2048, 512], P(None, 'var')
- grad_gain: float32 [2, 2, 512], P(None, None, 'var')
- grad_norm_bias: float32 [2, 2, 512], P(None, None, 'var')
Inputs may be any that keep to these rules, and one draw needn't show every extreme that they name: `counts`: in every aligned block of 12 windows one window has exactly 256 live variates. `row_index`: each window's list names every slot once; its first counts[w] entries are the live slots.
All inputs are finite; a program needn't handle non-finite values.
Results may differ from a plain program's by a relative error of at most 0.019.
Values may be sent and summed in bfloat16 or wider, within the bound.
A program may use at most 384 MiB of HBM per device.

v0:
```python
import jax
import jax.numpy as jnp
from jax import lax
from jax.sharding import PartitionSpec as P

HEADS = 8
LAYERS = 2


EPS = 1e-05


def layer_norm(values, gain, shift):
    centre = values - jnp.mean(values, axis=-1, keepdims=True)
    spread = jnp.mean(centre * centre, axis=-1, keepdims=True)
    return centre * lax.rsqrt(spread + EPS) * gain + shift


def smooth(values):
    return jax.nn.gelu(values, approximate=True)


def scores_of(query_heads, key_heads, key_valid, scale):
    raw = (
        jnp.einsum("wqhd,wkhd->whqk", query_heads, key_heads, preferred_element_type=jnp.float32)
        * scale
    )
    return jnp.where(key_valid[:, None, None, :], raw, -1e30)


def per_device(
    inputs,
    counts,
    row_index,
    w_qkv,
    bias_qv,
    w_attn_out,
    out_bias,
    w_in,
    bias_in,
    w_ffn_out,
    norm_gain,
    norm_bias,
    cotangent,
):
    wins, rows, width = inputs.shape
    cycle_size = lax.axis_size("var")
    length = rows * cycle_size
    first_row = lax.axis_index("var") * rows
    head_count = HEADS
    head_size = width // head_count
    scale = head_size ** (-0.5)
    flat = wins * rows
    slots = jnp.arange(length, dtype=jnp.int32)
    live = (slots[None, :] < counts[:, None]).astype(jnp.float32)
    window_ids = jnp.arange(wins, dtype=jnp.int32)[:, None]
    valid = jnp.zeros((wins, length), jnp.float32).at[window_ids, row_index].add(live)
    key_valid = valid > 0.5
    own_valid = lax.dynamic_slice_in_dim(valid, first_row, rows, 1).reshape(flat, 1)
    state = inputs.astype(jnp.float32).reshape(flat, width)
    kept = []
    for which_layer in range(LAYERS):
        x_low = state.astype(jnp.bfloat16)
        joint = jnp.dot(x_low, w_qkv[which_layer], preferred_element_type=jnp.float32)
        query = (joint[:, :width] + bias_qv[which_layer, :width]).astype(jnp.bfloat16)
        keys_low = joint[:, width : 2 * width].astype(jnp.bfloat16)
        values_low = (joint[:, 2 * width :] + bias_qv[which_layer, width:]).astype(jnp.bfloat16)
        pair = jnp.concatenate([keys_low, values_low], axis=1).reshape(wins, rows, 2 * width)
        whole = lax.all_gather(pair, "var", axis=1, tiled=True)
        query_heads = query.reshape(wins, rows, head_count, head_size)
        key_heads = whole[:, :, :width].reshape(wins, length, head_count, head_size)
        value_heads = whole[:, :, width:].reshape(wins, length, head_count, head_size)
        scores = scores_of(query_heads, key_heads, key_valid, scale)
        peak = jnp.max(scores, axis=-1, keepdims=True)
        expo = jnp.exp(scores - peak)
        total = jnp.sum(expo, axis=-1, keepdims=True)
        probs = expo / total
        top = peak + jnp.log(total)
        mixed = (
            jnp.einsum(
                "whqk,wkhd->wqhd",
                probs.astype(jnp.bfloat16),
                value_heads,
                preferred_element_type=jnp.float32,
            )
            .reshape(flat, width)
            .astype(jnp.bfloat16)
        )
        attn = (
            jnp.dot(mixed, w_attn_out[which_layer], preferred_element_type=jnp.float32)
            + out_bias[which_layer, 0]
        )
        normed, norm_one = jax.vjp(
            layer_norm, state + attn, norm_gain[which_layer, 0], norm_bias[which_layer, 0]
        )
        normed_low = normed.astype(jnp.bfloat16)
        hidden = (
            jnp.dot(normed_low, w_in[which_layer], preferred_element_type=jnp.float32)
            + bias_in[which_layer]
        )
        active, gelu_back = jax.vjp(smooth, hidden)
        active_low = active.astype(jnp.bfloat16)
        ffn = (
            jnp.dot(active_low, w_ffn_out[which_layer], preferred_element_type=jnp.float32)
            + out_bias[which_layer, 1]
        )
        state, norm_two = jax.vjp(
            layer_norm, normed + ffn, norm_gain[which_layer, 1], norm_bias[which_layer, 1]
        )
        stored = whole
        kept.append(
            (
                x_low,
                query_heads,
                stored,
                top,
                mixed,
                norm_one,
                normed_low,
                gelu_back,
                active_low,
                norm_two,
            )
        )
    layer_out = (state * own_valid).astype(jnp.bfloat16).reshape(wins, rows, width)
    grad = cotangent.astype(jnp.float32).reshape(flat, width) * own_valid
    collected = []
    for which_layer in reversed(range(LAYERS)):
        (
            x_low,
            query_heads,
            stored,
            top,
            mixed,
            norm_one,
            normed_low,
            gelu_back,
            active_low,
            norm_two,
        ) = kept[which_layer]
        dz_two, gain_two, shift_two = norm_two(grad)
        d_ffn = dz_two.astype(jnp.bfloat16)
        g_ffn_out = jnp.einsum("rf,rd->fd", active_low, d_ffn, preferred_element_type=jnp.float32)
        bias_two = jnp.sum(d_ffn.astype(jnp.float32), axis=0)
        d_active = jnp.einsum(
            "rd,fd->rf", d_ffn, w_ffn_out[which_layer], preferred_element_type=jnp.float32
        )
        (d_hidden,) = gelu_back(d_active)
        d_hidden = d_hidden.astype(jnp.bfloat16)
        g_in = jnp.einsum("rd,rf->df", normed_low, d_hidden, preferred_element_type=jnp.float32)
        g_bias_in = jnp.sum(d_hidden.astype(jnp.float32), axis=0)
        d_normed = dz_two + jnp.einsum(
            "rf,df->rd", d_hidden, w_in[which_layer], preferred_element_type=jnp.float32
        )
        dz_one, gain_one, shift_one = norm_one(d_normed)
        d_attn = dz_one.astype(jnp.bfloat16)
        g_attn_out = jnp.einsum("re,rd->ed", mixed, d_attn, preferred_element_type=jnp.float32)
        bias_one = jnp.sum(d_attn.astype(jnp.float32), axis=0)
        d_mixed = jnp.einsum(
            "rd,ed->re", d_attn, w_attn_out[which_layer], preferred_element_type=jnp.float32
        ).astype(jnp.bfloat16)
        whole = stored
        key_heads = whole[:, :, :width].reshape(wins, length, head_count, head_size)
        value_heads = whole[:, :, width:].reshape(wins, length, head_count, head_size)
        scores = scores_of(query_heads, key_heads, key_valid, scale)
        probs = jnp.exp(scores - top)
        grad_heads = d_mixed.reshape(wins, rows, head_count, head_size)
        d_probs = jnp.einsum(
            "wqhd,wkhd->whqk", grad_heads, value_heads, preferred_element_type=jnp.float32
        )
        centre = jnp.sum(probs * d_probs, axis=-1, keepdims=True)
        d_scores = (probs * (d_probs - centre)).astype(jnp.bfloat16)
        probs_low = probs.astype(jnp.bfloat16)
        d_query = (
            jnp.einsum("whqk,wkhd->wqhd", d_scores, key_heads, preferred_element_type=jnp.float32)
            * scale
        )
        d_query = d_query.reshape(flat, width).astype(jnp.bfloat16)
        span_rows = lax.axis_size("var") * rows
        d_key = (
            jnp.einsum("whqk,wqhd->kwhd", d_scores, query_heads, preferred_element_type=jnp.float32)
            * scale
        )
        d_value = jnp.einsum(
            "whqk,wqhd->kwhd", probs_low, grad_heads, preferred_element_type=jnp.float32
        )
        key_grads = lax.psum_scatter(
            jnp.concatenate(
                [d_key.reshape(span_rows, wins, width), d_value.reshape(span_rows, wins, width)],
                axis=2,
            ).astype(jnp.bfloat16),
            "var",
            scatter_dimension=0,
            tiled=True,
        ).astype(jnp.float32)
        key_grads = (
            jnp.transpose(key_grads, (1, 0, 2)).reshape(flat, 2 * width).astype(jnp.bfloat16)
        )
        d_joint = jnp.concatenate([d_query, key_grads], axis=1)
        g_qkv = jnp.einsum("rd,re->de", x_low, d_joint, preferred_element_type=jnp.float32)
        g_bias_qv = jnp.concatenate(
            [
                jnp.sum(d_query.astype(jnp.float32), axis=0),
                jnp.sum(key_grads[:, width:].astype(jnp.float32), axis=0),
            ]
        )
        grad = dz_one + jnp.einsum(
            "re,de->rd", d_joint, w_qkv[which_layer], preferred_element_type=jnp.float32
        )
        g_out_bias = jnp.stack([bias_one, bias_two])
        g_gain = jnp.stack([gain_one, gain_two])
        g_shift = jnp.stack([shift_one, shift_two])
        terms = (
            g_qkv,
            g_bias_qv,
            g_attn_out,
            g_out_bias,
            g_in,
            g_bias_in,
            g_ffn_out,
            g_gain,
            g_shift,
        )
        collected.append(terms)
    collected = collected[::-1]
    stacked = tuple((jnp.stack([entry[position] for entry in collected]) for position in range(9)))
    shards = (
        lax.psum_scatter(
            stacked[0].astype(jnp.bfloat16), "var", scatter_dimension=1, tiled=True
        ).astype(jnp.float32),
        lax.psum_scatter(
            stacked[1].astype(jnp.bfloat16), "var", scatter_dimension=1, tiled=True
        ).astype(jnp.float32),
        lax.psum_scatter(
            stacked[2].astype(jnp.bfloat16), "var", scatter_dimension=1, tiled=True
        ).astype(jnp.float32),
        lax.psum_scatter(
            stacked[3].astype(jnp.bfloat16), "var", scatter_dimension=2, tiled=True
        ).astype(jnp.float32),
        lax.psum_scatter(
            stacked[4].astype(jnp.bfloat16), "var", scatter_dimension=1, tiled=True
        ).astype(jnp.float32),
        lax.psum_scatter(
            stacked[5].astype(jnp.bfloat16), "var", scatter_dimension=1, tiled=True
        ).astype(jnp.float32),
        lax.psum_scatter(
            stacked[6].astype(jnp.bfloat16), "var", scatter_dimension=1, tiled=True
        ).astype(jnp.float32),
        lax.psum_scatter(
            stacked[7].astype(jnp.bfloat16), "var", scatter_dimension=2, tiled=True
        ).astype(jnp.float32),
        lax.psum_scatter(
            stacked[8].astype(jnp.bfloat16), "var", scatter_dimension=2, tiled=True
        ).astype(jnp.float32),
    )
    stacked = (
        lax.psum(shards[0].astype(jnp.bfloat16), "win").astype(jnp.float32),
        lax.psum(shards[1].astype(jnp.bfloat16), "win").astype(jnp.float32),
        lax.psum(shards[2].astype(jnp.bfloat16), "win").astype(jnp.float32),
        lax.psum(shards[3].astype(jnp.bfloat16), "win").astype(jnp.float32),
        lax.psum(shards[4].astype(jnp.bfloat16), "win").astype(jnp.float32),
        lax.psum(shards[5].astype(jnp.bfloat16), "win").astype(jnp.float32),
        lax.psum(shards[6].astype(jnp.bfloat16), "win").astype(jnp.float32),
        lax.psum(shards[7].astype(jnp.bfloat16), "win").astype(jnp.float32),
        lax.psum(shards[8].astype(jnp.bfloat16), "win").astype(jnp.float32),
    )
    grad_inputs = grad.reshape(wins, rows, width)
    return (
        layer_out,
        grad_inputs,
        stacked[0],
        stacked[1],
        stacked[2],
        stacked[3],
        stacked[4],
        stacked[5],
        stacked[6],
        stacked[7],
        stacked[8],
    )


def solution(mesh):
    return jax.shard_map(
        per_device,
        mesh=mesh,
        in_specs=(
            P("win", "var", None),
            P("win"),
            P("win", None),
            P(),
            P(),
            P(),
            P(),
            P(),
            P(),
            P(),
            P(),
            P(),
            P("win", "var", None),
        ),
        out_specs=(
            P("win", "var", None),
            P("win", "var", None),
            P(None, "var", None),
            P(None, "var"),
            P(None, "var", None),
            P(None, None, "var"),
            P(None, "var", None),
            P(None, "var"),
            P(None, "var", None),
            P(None, None, "var"),
            P(None, None, "var"),
        ),
        check_vma=False,
    )
```

profile of v0, /device:TPU:0, one launch (start us, length us, event | category | flops | bytes accessed | tf_op | source)
XLA Modules:
  0.0 852.6 jit_solution(17853859520514989682)
XLA Ops:
  13.5 21.7 %scatter_custom_fusion = f32[3072]{0:T(1024)S(1)} fusion(s32[3072]{0:T(1024)S(1)} %reshape.318, f32[3072]{0:T(1024)S(1)} %reshape.320, f32[]{:T(128)} %constant.20.clone.1), kind=kCustom, calls=%fused_computation.185 | custom fusion | flops 3072 | bytes 12292
  38.0 24.3 %all-gather.3.cloned.1.call-done = bf16[12,256,1024]{2,1,0:T(8,128)(2,1)} async-done(((bf16[12,64,1024]{2,1,0:T(8,128)(2,1)}), bf16[12,256,1024]{2,1,0:T(8,128)(2,1)}) %all-gather.3.cloned.1.call-update) | async-done | bytes 6291472 | tf_op jit(solution)/shard_map/all_gather | solution.py:69
  62.3 6.3 fusion.133
  106.0 43.7 %all-gather.5.cloned.1.call-done = bf16[12,256,1024]{2,1,0:T(8,128)(2,1)} async-done(((bf16[12,64,1024]{2,1,0:T(8,128)(2,1)}), bf16[12,256,1024]{2,1,0:T(8,128)(2,1)}) %all-gather.5.cloned.1.call-update) | async-done | bytes 6291472 | tf_op jit(solution)/shard_map/all_gather | solution.py:69
  149.7 6.1 fusion.132
  191.4 6.1 fusion.147
  208.3 6.4 fusion.32
  248.7 50.4 %reduce-scatter.24.cloned.1.call-done = bf16[64,12,1024]{2,0,1:T(8,128)(2,1)} async-done(((bf16[256,12,1024]{2,0,1:T(8,128)(2,1)}), bf16[64,12,1024]{2,0,1:T(8,128)(2,1)}) %reduce-scatter.24.cloned.1.call-update) | async-done | bytes 1572880 | tf_op jit(solution)/shard_map/reduce_scatter | solution.py:187
  306.1 7.7 fusion.148
  324.3 6.4 fusion.35
  369.4 45.7 %reduce-scatter.26.cloned.1.call-done = bf16[64,12,1024]{2,0,1:T(8,128)(2,1)} async-done(((bf16[256,12,1024]{2,0,1:T(8,128)(2,1)}), bf16[64,12,1024]{2,0,1:T(8,128)(2,1)}) %reduce-scatter.26.cloned.1.call-update) | async-done | bytes 1572880 | tf_op jit(solution)/shard_map/reduce_scatter | solution.py:187
  418.4 6.0 copy.83
  432.7 6.5 fusion.31
  439.2 6.0 fusion.30
  471.4 23.6 %reduce-scatter.28.cloned.1.call-done = bf16[2,128,512]{2,1,0:T(8,128)(2,1)} async-done(((bf16[2,512,512]{2,1,0:T(8,128)(2,1)}), bf16[2,128,512]{2,1,0:T(8,128)(2,1)}) %reduce-scatter.28.cloned.1.call-update) | async-done | bytes 262160 | tf_op jit(solution)/shard_map/reduce_scatter | solution.py:234
  494.9 47.1 %reduce-scatter.32.cloned.1.call-done = bf16[2,512,512]{2,1,0:T(8,128)(2,1)} async-done(((bf16[2,2048,512]{2,1,0:T(8,128)(2,1)}), bf16[2,512,512]{2,1,0:T(8,128)(2,1)}) %reduce-scatter.32.cloned.1.call-update) | async-done | bytes 1048592 | tf_op jit(solution)/shard_map/reduce_scatter | solution.py:246
  542.0 47.2 %reduce-scatter.30.cloned.1.call-done = bf16[2,128,2048]{2,1,0:T(8,128)(2,1)} async-done(((bf16[2,512,2048]{2,1,0:T(8,128)(2,1)}), bf16[2,128,2048]{2,1,0:T(8,128)(2,1)}) %reduce-scatter.30.cloned.1.call-update) | async-done | bytes 1048592 | tf_op jit(solution)/shard_map/reduce_scatter | solution.py:240
  589.2 22.0 %reduce-scatter.44.cloned.1.call-done = bf16[128,4]{1,0:T(8,128)(2,1)} async-done(((bf16[512,4]{1,0:T(8,128)(2,1)}), bf16[128,4]{1,0:T(8,128)(2,1)}) %reduce-scatter.44.cloned.1.call-update) | async-done | bytes 1040
  612.2 21.1 %reduce-scatter.42.cloned.1.call-done = bf16[128,4]{1,0:T(8,128)(2,1)} async-done(((bf16[512,4]{1,0:T(8,128)(2,1)}), bf16[128,4]{1,0:T(8,128)(2,1)}) %reduce-scatter.42.cloned.1.call-update) | async-done | bytes 1040
  634.2 21.1 %reduce-scatter.38.cloned.1.call-done = bf16[128,4]{1,0:T(8,128)(2,1)} async-done(((bf16[512,4]{1,0:T(8,128)(2,1)}), bf16[128,4]{1,0:T(8,128)(2,1)}) %reduce-scatter.38.cloned.1.call-update) | async-done | bytes 1040
  656.3 23.8 %reduce-scatter.40.cloned.1.call-done = bf16[512,2]{1,0:T(8,128)(2,1)} async-done(((bf16[2048,2]{1,0:T(8,128)(2,1)}), bf16[512,2]{1,0:T(8,128)(2,1)}) %reduce-scatter.40.cloned.1.call-update) | async-done | bytes 2064
  685.5 17.1 %reduce-scatter.36.cloned.1.call-done = bf16[256,2]{1,0:T(8,128)(2,1)} async-done(((bf16[1024,2]{1,0:T(8,128)(2,1)}), bf16[256,2]{1,0:T(8,128)(2,1)}) %reduce-scatter.36.cloned.1.call-update) | async-done | bytes 1040
  703.5 22.2 %all-reduce = (bf16[2,256]{1,0:T(2,128)(2,1)S(1)}, bf16[2,2,128]{2,1,0:T(2,128)(2,1)S(1)}, bf16[2,512]{1,0:T(2,128)(2,1)S(1)}, bf16[2,2,128]{2,1,0:T(2,128)(2,1)S(1)}, bf16[2,2,128]{2,1,0:T(2,128)(2,1)S(1)}) all-reduce(bf16[2,256]{1,0:T(2,128)(2,1)S(1)} %copy.86, ...), channel_id=1, replica_groups=mesh['win'=8,'var'=4] {'win'}, use_global_device_ids=true, to_apply=%region_32.33 | all-reduce | flops 3072 | bytes 12288 | tf_op jit(solution)/shard_map/psum | solution.py:258
  728.6 109.5 %all-reduce.4.cloned.1.call-done = (bf16[2,128,1536]{1,2,0:T(8,128)(2,1)}, bf16[2,128,512]{2,1,0:T(8,128)(2,1)}, bf16[2,128,2048]{2,1,0:T(8,128)(2,1)}, bf16[2,512,512]{2,1,0:T(8,128)(2,1)}) async-done(((bf16[2,128,1536]{1,2,0:T(8,128)(2,1)}, bf16[2,128,512]{2,1,0:T(8,128)(2,1)}, bf16[2,128,2048]{2,1,0:T(8,128)(2,1)}, bf16[2,512,512]{2,1,0:T(8,128)(2,1)}), (bf16[2,128,1536]{1,2,0:T(8,128)(2,1)}, ...) | async-done | bytes 3145744 | tf_op jit(solution)/shard_map/psum | solution.py:257
  (372 shorter events, 239.1 us)
Async XLA Ops:
  7.2 55.1 %all-gather.3.cloned.1.call-start = ((), (), s32[]{:S(2)}) async-start(), calls=%async_computation.11 | async-start | bytes 7864320 | tf_op jit(solution)/shard_map/all_gather | solution.py:69
  13.1 24.8 %copy-start.60 = (f32[2,2,512]{2,1,0:T(2,128)S(1)}, f32[2,2,512]{2,1,0:T(2,128)}, u32[]{:S(2)}) copy-start(f32[2,2,512]{2,1,0:T(2,128)} %param.24) | copy-start | bytes 24580
  13.1 24.9 %copy-start.57 = (f32[2,2048]{1,0:T(2,128)S(1)}, f32[2,2048]{1,0:T(2,128)}, u32[]{:S(2)}) copy-start(f32[2,2048]{1,0:T(2,128)} %param.21) | copy-start | bytes 49156
  13.1 136.6 %all-gather.5.cloned.1.call-start = ((), (), s32[]{:S(2)}) async-start(), calls=%async_computation.12 | async-start | bytes 7864320 | tf_op jit(solution)/shard_map/all_gather | solution.py:69
  37.9 57.3 %copy-start.52 = (f32[1,1,512]{2,1,0:T(1,128)}, f32[1,1,512]{2,1,0:T(1,128)S(1)}, u32[]{:S(2)}) copy-start(f32[1,1,512]{2,1,0:T(1,128)S(1)} %get-tuple-element.97) | copy-start | bytes 6148
  37.9 146.2 %copy-start.54 = (f32[1,1,512]{2,1,0:T(1,128)}, f32[1,1,512]{2,1,0:T(1,128)S(1)}, u32[]{:S(2)}) copy-start(f32[1,1,512]{2,1,0:T(1,128)S(1)} %get-tuple-element.98) | copy-start | bytes 6148
  103.2 196.0 %reduce-scatter.24.cloned.1.call-start = ((), (), s32[]{:S(2)}) async-start(), calls=%async_computation.13 | async-start | bytes 7864320 | tf_op jit(solution)/shard_map/reduce_scatter | solution.py:187
  103.3 52.6 %copy-start.50 = (f32[12,64]{1,0:T(8,128)}, f32[12,64]{1,0:T(8,128)S(1)}, u32[]{:S(2)}) copy-start(f32[12,64]{1,0:T(8,128)S(1)} %constant_dynamic-slice_fusion) | copy-start | bytes 9220
  240.6 174.5 %reduce-scatter.26.cloned.1.call-start = ((), (), s32[]{:S(2)}) async-start(), calls=%async_computation.14 | async-start | bytes 7864320 | tf_op jit(solution)/shard_map/reduce_scatter | solution.py:187
  245.4 53.8 %copy-start.25 = (f32[768,512]{1,0:T(8,128)S(1)}, f32[768,512]{1,0:T(8,128)}, u32[]{:S(2)}) copy-start(f32[768,512]{1,0:T(8,128)} %copy-done.23) | copy-start | bytes 4718596
  356.6 110.3 %reduce-scatter.34.cloned.1.call-start = ((), (), s32[]{:S(2)}) async-start(), calls=%async_computation.18 | async-start | bytes 3932160
  364.3 50.8 %copy-start.38 = (bf16[768,512]{1,0:T(8,128)(2,1)S(1)}, bf16[768,512]{1,0:T(8,128)(2,1)}, u32[]{:S(2)}) copy-start(bf16[768,512]{1,0:T(8,128)(2,1)} %convert_element_type.271) | copy-start | bytes 2359300
  364.3 50.8 %copy-start.75 = (bf16[12,64,512]{2,1,0:T(8,128)(2,1)S(1)}, bf16[12,64,512]{2,1,0:T(8,128)(2,1)}, u32[]{:S(2)}) copy-start(bf16[12,64,512]{2,1,0:T(8,128)(2,1)} %param.13) | copy-start | bytes 2359300
  428.8 66.2 %reduce-scatter.28.cloned.1.call-start = ((), (), s32[]{:S(2)}) async-start(), calls=%async_computation.15 | async-start | bytes 1310720 | tf_op jit(solution)/shard_map/reduce_scatter | solution.py:234
  432.4 109.6 %reduce-scatter.32.cloned.1.call-start = ((), (), s32[]{:S(2)}) async-start(), calls=%async_computation.17 | async-start | bytes 5242880 | tf_op jit(solution)/shard_map/reduce_scatter | solution.py:246
  447.5 141.7 %reduce-scatter.30.cloned.1.call-start = ((), (), s32[]{:S(2)}) async-start(), calls=%async_computation.16 | async-start | bytes 5242880 | tf_op jit(solution)/shard_map/reduce_scatter | solution.py:240
  457.5 153.8 %reduce-scatter.44.cloned.1.call-start = ((), (), s32[]{:S(2)}) async-start(), calls=%async_computation.23 | async-start | bytes 163840
  461.4 171.8 %reduce-scatter.42.cloned.1.call-start = ((), (), s32[]{:S(2)}) async-start(), calls=%async_computation.22 | async-start | bytes 163840
  462.6 192.7 %reduce-scatter.38.cloned.1.call-start = ((), (), s32[]{:S(2)}) async-start(), calls=%async_computation.20 | async-start | bytes 163840
  463.8 216.3 %reduce-scatter.40.cloned.1.call-start = ((), (), s32[]{:S(2)}) async-start(), calls=%async_computation.21 | async-start | bytes 655360
  465.0 237.6 %reduce-scatter.36.cloned.1.call-start = ((), (), s32[]{:S(2)}) async-start(), calls=%async_computation.19 | async-start | bytes 327680
  466.2 214.9 %copy-start.28 = (f32[768,512]{1,0:T(8,128)S(1)}, f32[768,512]{1,0:T(8,128)}, u32[]{:S(2)}) copy-start(f32[768,512]{1,0:T(8,128)} %copy-done.27) | copy-start | bytes 4718596
  466.2 214.9 %copy-start.39 = (bf16[768,512]{1,0:T(8,128)(2,1)S(1)}, bf16[768,512]{1,0:T(8,128)(2,1)}, u32[]{:S(2)}) copy-start(bf16[768,512]{1,0:T(8,128)(2,1)} %convert_element_type.271) | copy-start | bytes 2359300
  466.2 371.9 %all-reduce.4.cloned.1.call-start = ((), (), s32[]{:S(2)}) async-start(), calls=%async_computation.24 | async-start | bytes 6291456 | tf_op jit(solution)/shard_map/psum | solution.py:257
  (72 other events, 330.0 us)
Sparse Core Ops, SparseCore 0:
  13.2 49.0 all-gather.2
  103.3 46.3 all-gather.4
  240.8 58.3 reduce-scatter.23
  356.7 58.3 reduce-scatter.25
  428.9 37.9 reduce-scatter.33
  470.0 24.9 reduce-scatter.27
  497.5 44.4 reduce-scatter.31
  544.7 44.4 reduce-scatter.29
  591.7 19.5 reduce-scatter.43
  613.7 19.5 reduce-scatter.41
  635.7 19.5 reduce-scatter.37
  658.4 21.6 reduce-scatter.39
  682.5 20.0 reduce-scatter.35
  707.4 130.6 all-reduce.3
where the time goes:
time: 861 us; the launch traced here: 853 us
  waiting for transfers between devices  497 us (58%)
  local copies, waits for them, and re-layouts  121 us (14%)
  matrix products  120 us (14%)
  other arithmetic  75.5 us (9%)
  blocking collectives  22.2 us (3%)
  between operations  15.6 us (2%)
    psum x1, waiting for transfers between devices, per_device(): lax.psum(shards[0].astype(jnp.bfloat16), 'win').astype(jnp.float32)  110 us
    unnamed x20, waiting for transfers between devices  106 us
    reduce_scatter x2, waiting for transfers between devices, per_device(): lax.psum_scatter(jnp.concatenate([d_key.reshape(span_rows, wins, width),...  96.1 us
    all_gather x2, waiting for transfers between devices, per_device(): whole = lax.all_gather(pair, 'var', axis=1, tiled=True)  68 us
    reduce_scatter x1, waiting for transfers between devices, per_device(): lax.psum_scatter(stacked[4].astype(jnp.bfloat16), 'var', scatter_dimensio...  47.2 us
    reduce_scatter x1, waiting for transfers between devices, per_device(): lax.psum_scatter(stacked[6].astype(jnp.bfloat16), 'var', scatter_dimensio...  47.1 us
    unnamed x186, local copies, waits for them, and re-layouts  47 us
    reduce_scatter x1, waiting for transfers between devices, per_device(): lax.psum_scatter(stacked[2].astype(jnp.bfloat16), 'var', scatter_dimensio...  23.6 us
  transfers between devices with their start and end apart: 14, of which 14 were waited for; matrix products, arithmetic and copies ran while one was open for 11% of the time, Pallas kernels for 0%

commit v1 on v0

--- a/solution.py
+++ b/solution.py
@@ -1,6 +1,10 @@
+import functools
+
 import jax
 import jax.numpy as jnp
 from jax import lax
+from jax.experimental import pallas as pl
+from jax.experimental.pallas import tpu as pltpu
 from jax.sharding import PartitionSpec as P
 
 HEADS = 8
@@ -8,6 +12,12 @@
 
 
 EPS = 1e-05
+LOW = jnp.bfloat16
+F32 = jnp.float32
+MESH = pl.DeviceIdType.MESH
+VMEM_BYTES = 60 << 20
+SMOOTH = 0.7978845608028654
+CUBIC = 0.044715
 
 
 def layer_norm(values, gain, shift):
@@ -280,9 +290,922 @@
     )
 
 
+def dot(left, right, left_dim, right_dim):
+    return lax.dot_general(
+        left, right, (((left_dim,), (right_dim,)), ((), ())), preferred_element_type=F32
+    )
+
+
+def flip(index, bit):
+    return index + bit - 2 * bit * lax.rem(index // bit, 2)
+
+
+def half_of(index, bit):
+    return lax.rem(index // bit, 2)
+
+
+def partner(axis, bit):
+    win, var = lax.axis_index("win"), lax.axis_index("var")
+    if axis == "win":
+        return (flip(win, bit), var)
+    return (win, flip(var, bit))
+
+
+def greet(partners):
+    barrier = pltpu.get_barrier_semaphore()
+    for other in partners:
+        pl.semaphore_signal(barrier, inc=1, device_id=other, device_id_type=MESH)
+    pl.semaphore_wait(barrier, len(partners))
+
+
+def assign(counts, wins, owners):
+    each = wins // owners
+    keys = [counts[w] * wins + w for w in range(wins)]
+    for stop in range(wins - 1, 0, -1):
+        for low in range(stop):
+            first, second = keys[low], keys[low + 1]
+            keys[low], keys[low + 1] = jnp.maximum(first, second), jnp.minimum(first, second)
+    load = [jnp.int32(0)] * owners
+    held = [jnp.int32(0)] * owners
+    slots, names = [], []
+    for key in keys:
+        count, name = key // wins, lax.rem(key, wins)
+        best, which = load[0] + (held[0] // each) * 1000000, jnp.int32(0)
+        for owner in range(1, owners):
+            price = load[owner] + (held[owner] // each) * 1000000
+            better = price < best
+            best = jnp.where(better, price, best)
+            which = jnp.where(better, owner, which)
+        slot = jnp.int32(0)
+        for owner in range(owners):
+            mine = which == owner
+            slot = jnp.where(mine, owner * each + held[owner], slot)
+            load[owner] = jnp.where(mine, load[owner] + ((count + 15) // 16) * 16, load[owner])
+            held[owner] = jnp.where(mine, held[owner] + 1, held[owner])
+        slots.append(slot)
+        names.append(name)
+    order = []
+    for place in range(wins):
+        window = jnp.int32(0)
+        for slot, name in zip(slots, names):
+            window = jnp.where(slot == place, name, window)
+        order.append(window)
+    return order
+
+
+def spread_kernel(
+    owners, counts, x, g, x_out, g_out, meta, x_stage, g_stage, x_send, x_recv, g_send, g_recv, own_sem
+):
+    wins, rows = x.shape[0], x.shape[1]
+    each = wins // owners
+    me = lax.axis_index("var")
+    others = [flip(me, 1), flip(me, 2), flip(flip(me, 1), 2)]
+    win = lax.axis_index("win")
+    barrier = pltpu.get_barrier_semaphore()
+    for other in others:
+        pl.semaphore_signal(barrier, inc=1, device_id=(win, other), device_id_type=MESH)
+    order = assign(counts, wins, owners)
+    for place in range(wins):
+        meta[place] = order[place]
+        x_stage[place] = x[order[place]]
+    pl.semaphore_wait(barrier, len(others))
+
+    def copies(stage, out, send, recv):
+        sent = []
+        for place, other in enumerate(others):
+            sent.append(
+                pltpu.make_async_remote_copy(
+                    src_ref=stage.at[pl.ds(other * each, each)],
+                    dst_ref=out.at[:, pl.ds(pl.multiple_of(me * rows, rows), rows), :],
+                    send_sem=send.at[place],
+                    recv_sem=recv.at[place],
+                    device_id=(win, other),
+                    device_id_type=MESH,
+                )
+            )
+        return sent
+
+    x_sent = copies(x_stage, x_out, x_send, x_recv)
+    for copy in x_sent:
+        copy.start()
+    for place in range(wins):
+        g_stage[place] = g[order[place]]
+    g_sent = copies(g_stage, g_out, g_send, g_recv)
+    for copy in g_sent:
+        copy.start()
+    own = pl.ds(pl.multiple_of(me * rows, rows), rows)
+    own_x = pltpu.make_async_copy(
+        x_stage.at[pl.ds(me * each, each)], x_out.at[:, own, :], own_sem.at[0]
+    )
+    own_g = pltpu.make_async_copy(
+        g_stage.at[pl.ds(me * each, each)], g_out.at[:, own, :], own_sem.at[1]
+    )
+    own_x.start()
+    own_g.start()
+    total = jnp.int32(0)
+    for place in range(each):
+        name = jnp.int32(0)
+        for owner in range(owners):
+            name = jnp.where(me == owner, order[owner * each + place], name)
+        meta[wins + place] = name
+        meta[wins + each + place] = counts[name]
+        total = total + ((counts[name] + 15) // 16) * 16
+    meta[wins + 2 * each] = me
+    meta[wins + 2 * each + 1] = total
+    own_x.wait()
+    own_g.wait()
+    for copy in x_sent + g_sent:
+        copy.wait()
+
+
+class Plan:
+    def __init__(self, meta, wins, each):
+        self.names = [meta[wins + place] for place in range(each)]
+        self.counts = [meta[wins + each + place] for place in range(each)]
+        self.starts = []
+        total = jnp.int32(0)
+        for count in self.counts:
+            self.starts.append(total)
+            total = total + ((count + 15) // 16) * 16
+        self.total = total
+        self.tall = jnp.logical_or(jnp.logical_and(total > 256, total <= 384), total > 512)
+        self.blocks = jnp.where(total <= 384, 1, 2)
+
+    def each_block(self, body):
+        for size in (256, 384):
+
+            @pl.when(self.tall if size == 384 else jnp.logical_not(self.tall))
+            def _(size=size):
+                def step(block, carry):
+                    body(size, block, pl.ds(pl.multiple_of(block * size, 128), size))
+                    return carry
+
+                lax.fori_loop(0, self.blocks, step, 0)
+
+    def pick(self, values, window):
+        chosen = values[0]
+        for place in range(1, len(values)):
+            chosen = jnp.where(window == place, values[place], chosen)
+        return chosen
+
+    def each_window(self, body):
+        def step(window, carry):
+            count = self.pick(self.counts, window)
+            start = pl.multiple_of(self.pick(self.starts, window), 16)
+            for size in (64, 128, 192, 256):
+
+                @pl.when(jnp.logical_and(count <= size, count > size - 64))
+                def _(size=size):
+                    body(size, count, pl.ds(start, size))
+
+            return carry
+
+        lax.fori_loop(0, len(self.counts), step, 0)
+
+
+def marks(row_index, name, count, length):
+    listed = row_index[pl.ds(name, 1), :]
+    slot = lax.broadcasted_iota(jnp.int32, (length, length), 0)
+    place = lax.broadcasted_iota(jnp.int32, (length, length), 1)
+    hit = jnp.logical_and(slot == listed, place < count)
+    return jnp.where(hit, 1.0, 0.0).astype(LOW)
+
+
+def mean_of(values):
+    return jnp.mean(values, axis=-1, keepdims=True)
+
+
+def normalize(values):
+    centre = values - mean_of(values)
+    inverse = lax.rsqrt(mean_of(centre * centre) + EPS)
+    return centre * inverse, inverse
+
+
+def normalize_back(grad, gain, normal, inverse):
+    scaled = grad * gain
+    return inverse * (scaled - mean_of(scaled) - normal * mean_of(scaled * normal))
+
+
+def two_heads(pair, lane_low, lane_high):
+    return jnp.concatenate([pair * lane_low, pair * lane_high], axis=0)
+
+
+def lane_masks(lanes):
+    lane = lax.broadcasted_iota(jnp.int32, (1, lanes), 1)
+    low = jnp.where(lane < lanes // 2, 1.0, 0.0)
+    return low.astype(LOW), (1.0 - low).astype(LOW)
+
+
+def join_heads(stacked):
+    size, lanes = stacked.shape[0] // 2, stacked.shape[1]
+    lane = lax.broadcasted_iota(jnp.int32, (size, lanes), 1)
+    return jnp.where(lane < lanes // 2, stacked[:size], stacked[size:])
+
+
+def forward_kernel(
+    meta, row_index, x, w_qkv, w_attn, w_in, w_out, bias_qv, out_bias, bias_in, gain, shift,
+    lefts_out, qkv_out, slope_out, normal_out, inverse_out, top_out, layer_out,
+    wv_qkv, wv_attn, wv_in, wv_out, lefts, qkv, slope, normal, inverse, top, state,
+    weight_sem, out_sem,
+):
+    each, length, width = x.shape
+    wins = row_index.shape[0]
+    layers = w_qkv.shape[0]
+    hidden_width = w_in.shape[2]
+    pieces = hidden_width // width
+    part = width // pieces
+    plan = Plan(meta, wins, each)
+    weights = ((w_qkv, wv_qkv), (w_attn, wv_attn), (w_in, wv_in), (w_out, wv_out))
+
+    def fetch(layer, which):
+        source, target = weights[which]
+        return pltpu.make_async_copy(
+            source.at[layer], target.at[layer], weight_sem.at[layer, which]
+        )
+
+    for layer in range(layers):
+        for which in range(4):
+            fetch(layer, which).start()
+
+    state[...] = jnp.zeros_like(state)
+    for layer in range(layers):
+        lefts[layer, 1] = jnp.zeros(lefts.shape[2:], LOW)
+        qkv[layer] = jnp.zeros(qkv.shape[1:], LOW)
+    for place in range(each):
+        hits = marks(row_index, plan.names[place], plan.counts[place], length)
+        start = pl.multiple_of(plan.starts[place], 16)
+        state[pl.ds(start, length), :] = dot(hits, x[place], 0, 0)
+
+    kept = (
+        (lefts, lefts_out, lambda ref, layer, rows: ref.at[layer, :, rows, :]),
+        (qkv, qkv_out, lambda ref, layer, rows: ref.at[layer, rows, :]),
+        (slope, slope_out, lambda ref, layer, rows: ref.at[layer, rows, :]),
+        (normal, normal_out, lambda ref, layer, rows: ref.at[layer, :, rows, :]),
+        (inverse, inverse_out, lambda ref, layer, rows: ref.at[layer, rows, :]),
+        (top, top_out, lambda ref, layer, rows: ref.at[layer, rows, :]),
+    )
+
+    def stores(layer, block, rows):
+        return [
+            pltpu.make_async_copy(
+                view(source, layer, rows), view(target, layer, rows), out_sem.at[layer, which, block]
+            )
+            for which, (source, target, view) in enumerate(kept)
+        ]
+
+    lane_low, lane_high = lane_masks(128)
+
+    def one_layer(layer, carry):
+        fetch(layer, 0).wait()
+
+        def project(size, block, rows):
+            tokens = state[rows, :].astype(LOW)
+            lefts[layer, 0, rows, :] = tokens
+            for which in range(3):
+                columns = slice(which * width, (which + 1) * width)
+                joint = dot(tokens, wv_qkv[layer, :, columns], 1, 0)
+                if which == 0:
+                    joint = (joint + bias_qv[pl.ds(layer, 1), :width]).astype(LOW) * LOW(0.125)
+                elif which == 2:
+                    joint = (joint + bias_qv[pl.ds(layer, 1), width:]).astype(LOW)
+                else:
+                    joint = joint.astype(LOW)
+                qkv[layer, rows, columns] = joint
+
+        plan.each_block(project)
+
+        def attend(size, count, rows):
+            column = lax.broadcasted_iota(jnp.int32, (2 * size, size), 1)
+            live = column < count
+
+            def pair(which, carry):
+                at = pl.multiple_of(which * 128, 128)
+                query = two_heads(qkv[layer, rows, pl.ds(at, 128)], lane_low, lane_high)
+                key = qkv[layer, rows, pl.ds(pl.multiple_of(at + width, 128), 128)]
+                value = qkv[layer, rows, pl.ds(pl.multiple_of(at + 2 * width, 128), 128)]
+                scores = jnp.where(live, dot(query, key, 1, 1), -1e30)
+                peak = jnp.max(scores, axis=-1, keepdims=True)
+                expo = jnp.exp(scores - peak)
+                total = jnp.sum(expo, axis=-1, keepdims=True)
+                probs = (expo * (1.0 / total)).astype(LOW)
+                lefts[layer, 1, rows, pl.ds(at, 128)] = join_heads(dot(probs, value, 1, 0)).astype(LOW)
+                logs = jnp.broadcast_to(peak + jnp.log(total), (2 * size, 128))
+                top[layer, rows, pl.ds(at, 128)] = join_heads(logs)
+                return carry
+
+            lax.fori_loop(0, width // 128, pair, 0)
+
+        plan.each_window(attend)
+        for which in range(1, 4):
+            fetch(layer, which).wait()
+
+        def feed(size, block, rows):
+            first = dot(lefts[layer, 1, rows, :], wv_attn[layer], 1, 0) + out_bias[layer, 0:1, :]
+            one, inverse_one = normalize(state[rows, :] + first)
+            normal[layer, 0, rows, :] = one
+            after = one * gain[layer, 0:1, :] + shift[layer, 0:1, :]
+            after_low = after.astype(LOW)
+            lefts[layer, 2, rows, :] = after_low
+            second = jnp.zeros((size, width), F32)
+            for piece in range(pieces):
+                columns = slice(piece * width, (piece + 1) * width)
+                hidden = dot(after_low, wv_in[layer, :, columns], 1, 0) + bias_in[pl.ds(layer, 1), columns]
+                squared = hidden * hidden
+                bend = jnp.tanh(SMOOTH * hidden * (1.0 + CUBIC * squared))
+                half = 0.5 * (1.0 + bend)
+                active = (hidden * half).astype(LOW)
+                rise = half + 0.5 * hidden * (1.0 - bend * bend) * (
+                    SMOOTH * (1.0 + 3.0 * CUBIC * squared)
+                )
+                slope[layer, rows, columns] = rise.astype(LOW)
+                for sub in range(pieces):
+                    lefts[layer, 3 + sub, rows, piece * part : (piece + 1) * part] = active[
+                        :, sub * part : (sub + 1) * part
+                    ]
+                second = second + dot(active, wv_out[layer, columns, :], 1, 0)
+            two, inverse_two = normalize(after + second + out_bias[layer, 1:2, :])
+            normal[layer, 1, rows, :] = two
+            state[rows, :] = two * gain[layer, 1:2, :] + shift[layer, 1:2, :]
+            lane = lax.broadcasted_iota(jnp.int32, (size, 128), 1)
+            inverse[layer, rows, :] = jnp.where(lane < 64, inverse_one, inverse_two)
+            for copy in stores(layer, block, rows):
+                copy.start()
+
+        plan.each_block(feed)
+        return carry
+
+    lax.fori_loop(0, layers, one_layer, 0)
+    for place in range(each):
+        hits = marks(row_index, plan.names[place], plan.counts[place], length)
+        start = pl.multiple_of(plan.starts[place], 16)
+        layer_out[place] = dot(hits, state[pl.ds(start, length), :].astype(LOW), 1, 0).astype(LOW)
+
+    for layer in range(layers):
+
+        def finish(size, block, rows, layer=layer):
+            for copy in stores(layer, block, rows):
+                copy.wait()
+
+        plan.each_block(finish)
+
+
+def backward_kernel(
+    meta, row_index, g, w_qkv, w_attn, w_in, w_out, gain,
+    qkv_in, slope_in, normal_in, inverse_in, top_in,
+    rights_out, grad_out, sums,
+    wv_qkv, wv_attn, wv_in, wv_out, rights, qkv, slope, normal, inverse, top, state, mixed_grad,
+    weight_sem, in_sem, out_sem,
+):
+    each, length, width = g.shape
+    wins = row_index.shape[0]
+    layers = w_qkv.shape[0]
+    hidden_width = w_in.shape[2]
+    pieces = hidden_width // width
+    plan = Plan(meta, wins, each)
+    weights = ((w_out, wv_out), (w_in, wv_in), (w_attn, wv_attn), (w_qkv, wv_qkv))
+
+    def fetch(layer, which):
+        source, target = weights[which]
+        return pltpu.make_async_copy(
+            source.at[layer], target.at[layer], weight_sem.at[layer, which]
+        )
+
+    kept = (
+        (normal_in, normal, lambda ref, layer, rows: ref.at[layer, :, rows, :]),
+        (inverse_in, inverse, lambda ref, layer, rows: ref.at[layer, rows, :]),
+        (slope_in, slope, lambda ref, layer, rows: ref.at[layer, rows, :]),
+        (qkv_in, qkv, lambda ref, layer, rows: ref.at[layer, rows, :]),
+        (top_in, top, lambda ref, layer, rows: ref.at[layer, rows, :]),
+    )
+
+    def loads(layer, block, rows):
+        return [
+            pltpu.make_async_copy(
+                view(source, layer, rows), view(target, layer, rows), in_sem.at[layer, which, block]
+            )
+            for which, (source, target, view) in enumerate(kept)
+        ]
+
+    for layer in range(layers):
+        qkv[layer, 256:] = jnp.zeros((qkv.shape[1] - 256, qkv.shape[2]), LOW)
+    for layer in reversed(range(layers)):
+
+        def begin(size, block, rows, layer=layer):
+            for copy in loads(layer, block, rows):
+                copy.start()
+
+        fetch(layer, 0).start()
+        plan.each_block(begin)
+        for which in range(1, 4):
+            fetch(layer, which).start()
+
+    state[...] = jnp.zeros_like(state)
+    mixed_grad[...] = jnp.zeros_like(mixed_grad)
+    sums[...] = jnp.zeros_like(sums)
+    for layer in range(layers):
+        rights[layer, 0:3] = jnp.zeros((3,) + rights.shape[2:], LOW)
+    for place in range(each):
+        hits = marks(row_index, plan.names[place], plan.counts[place], length)
+        start = pl.multiple_of(plan.starts[place], 16)
+        state[pl.ds(start, length), :] = dot(hits, g[place], 0, 0)
+
+    lane_low, lane_high = lane_masks(128)
+
+    def add_rows(layer, place, values):
+        sums[layer, place : place + 1, :] += jnp.sum(values, axis=0, keepdims=True)
+
+    def one_layer(step, carry):
+        layer = layers - 1 - step
+        for which in range(3):
+            fetch(layer, which).wait()
+
+        def feed(size, block, rows):
+            for copy in loads(layer, block, rows):
+                copy.wait()
+            grad = state[rows, :]
+            two = normal[layer, 1, rows, :]
+            add_rows(layer, 9, grad * two)
+            add_rows(layer, 11, grad)
+            back = normalize_back(grad, gain[layer, 1:2, :], two, inverse[layer, rows, 64:65])
+            back_low = back.astype(LOW)
+            rights[layer, 8, rows, :] = back_low
+            add_rows(layer, 3, back_low.astype(F32))
+            for piece in range(pieces):
+                columns = slice(piece * width, (piece + 1) * width)
+                active = dot(back_low, wv_out[layer, columns, :], 1, 1)
+                hidden = (active * slope[layer, rows, columns].astype(F32)).astype(LOW)
+                rights[layer, 4 + piece, rows, :] = hidden
+                add_rows(layer, 4 + piece, hidden.astype(F32))
+                back = back + dot(hidden, wv_in[layer, :, columns], 1, 1)
+            one = normal[layer, 0, rows, :]
+            add_rows(layer, 8, back * one)
+            add_rows(layer, 10, back)
+            back = normalize_back(back, gain[layer, 0:1, :], one, inverse[layer, rows, 0:1])
+            back_low = back.astype(LOW)
+            rights[layer, 3, rows, :] = back_low
+            add_rows(layer, 2, back_low.astype(F32))
+            mixed_grad[rows, :] = dot(back_low, wv_attn[layer], 1, 1).astype(LOW)
+            state[rows, :] = back
+
+        plan.each_block(feed)
+
+        def attend(size, count, rows):
+            row = lax.broadcasted_iota(jnp.int32, (2 * size, size), 0)
+            column = lax.broadcasted_iota(jnp.int32, (2 * size, size), 1)
+            row = jnp.where(row < size, row, row - size)
+            live = jnp.logical_and(column < count, row < count)
+
+            def pair(which, carry):
+                at = pl.multiple_of(which * 128, 128)
+                query = two_heads(qkv[layer, rows, pl.ds(at, 128)], lane_low, lane_high)
+                key = qkv[layer, rows, pl.ds(pl.multiple_of(at + width, 128), 128)]
+                value = qkv[layer, rows, pl.ds(pl.multiple_of(at + 2 * width, 128), 128)]
+                grad = two_heads(mixed_grad[rows, pl.ds(at, 128)], lane_low, lane_high)
+                logs = top[layer, rows, pl.ds(at, 128)]
+                logs = jnp.concatenate([logs[:, 0:1], logs[:, 64:65]], axis=0)
+                probs = jnp.where(live, jnp.exp(dot(query, key, 1, 1) - logs), 0.0)
+                d_probs = dot(grad, value, 1, 1)
+                centre = jnp.sum(probs * d_probs, axis=-1, keepdims=True)
+                d_scores = (probs * (d_probs - centre)).astype(LOW)
+                d_query = join_heads(dot(d_scores, key, 1, 0)) * 0.125
+                rights[layer, 0, rows, pl.ds(at, 128)] = d_query.astype(LOW)
+                rights[layer, 1, rows, pl.ds(at, 128)] = dot(d_scores, query, 0, 0).astype(LOW)
+                rights[layer, 2, rows, pl.ds(at, 128)] = dot(probs.astype(LOW), grad, 0, 0).astype(LOW)
+                return carry
+
+            lax.fori_loop(0, width // 128, pair, 0)
+
+        plan.each_window(attend)
+        fetch(layer, 3).wait()
+
+        def project(size, block, rows):
+            grad = state[rows, :]
+            for which in range(3):
+                columns = slice(which * width, (which + 1) * width)
+                piece = rights[layer, which, rows, :]
+                grad = grad + dot(piece, wv_qkv[layer, :, columns], 1, 1)
+                if which != 1:
+                    add_rows(layer, which // 2, piece.astype(F32))
+            state[rows, :] = grad
+            pltpu.make_async_copy(
+                rights.at[layer, :, rows, :], rights_out.at[layer, :, rows, :], out_sem.at[layer, block]
+            ).start()
+
+        plan.each_block(project)
+        return carry
+
+    lax.fori_loop(0, layers, one_layer, 0)
+    for place in range(each):
+        hits = marks(row_index, plan.names[place], plan.counts[place], length)
+        start = pl.multiple_of(plan.starts[place], 16)
+        grad_out[place] = dot(hits, state[pl.ds(start, length), :].astype(LOW), 1, 0).astype(LOW)
+
+    for layer in range(layers):
+
+        def finish(size, block, rows, layer=layer):
+            pltpu.make_async_copy(
+                rights.at[layer, :, rows, :], rights_out.at[layer, :, rows, :], out_sem.at[layer, block]
+            ).wait()
+
+        plan.each_block(finish)
+
+
+LAGS = (0, 1, 3, 4, 5, 6, 7, 8, 9)
+ROUTE = (("var", 1), ("var", 2), ("win", 1), ("win", 2), ("win", 4))
+
+
+def merge_kernel(
+    owners, meta, lefts, rights, sums, layer_out, grad,
+    merged, sums_out, layer_back, grad_back,
+    left_in, right_in, part, got_core, hold_x, got_x, hold_y, got_y, hold_a, got_a, hold_b, got_b,
+    whole, sums_hold, sums_got,
+    in_sem, send_sem, recv_sem, out_sem, sums_send, sums_recv, back_send, back_recv, own_sem,
+):
+    chunks = merged.shape[0]
+    layers = lefts.shape[0]
+    per_layer = chunks // layers
+    packed, width = left_in.shape[1], left_in.shape[2]
+    part_rows = part.shape[3]
+    each = layer_out.shape[0]
+    rows = layer_back.shape[1]
+    win, var = lax.axis_index("win"), lax.axis_index("var")
+    core, x_half = half_of(var, 1), half_of(var, 2)
+    y_half, a_half, b_half = half_of(win, 1), half_of(win, 2), half_of(win, 4)
+    others = [flip(var, 1), flip(var, 2), flip(flip(var, 1), 2)]
+    route = [partner(axis, bit) for axis, bit in ROUTE]
+    greet(route + [(win, others[2])])
+    total = meta[meta.shape[0] - 1]
+
+    def block_of(chunk):
+        layer, place = layers - 1 - chunk // per_layer, lax.rem(chunk, per_layer)
+        late = (place + 4) // 8
+        far = place // 8
+        left = (1 - late) * (place // 3) + late * (2 + far * (lax.rem(place, 8) + 1))
+        right = place - far * lax.rem(place, 8)
+        return layer, left, right
+
+    def loads(chunk):
+        layer, left, right = block_of(chunk)
+        slot = lax.rem(chunk, 2)
+        return (
+            pltpu.make_async_copy(lefts.at[layer, left], left_in.at[slot], in_sem.at[0, slot]),
+            pltpu.make_async_copy(rights.at[layer, right], right_in.at[slot], in_sem.at[1, slot]),
+        )
+
+    quarter = part_rows // 2
+    eighth = quarter // 2
+    sixteenth = eighth // 2
+    at_y = pl.multiple_of(y_half * quarter, sixteenth)
+    at_a = pl.multiple_of(at_y + a_half * eighth, sixteenth)
+    at_b = pl.multiple_of(at_a + b_half * sixteenth, sixteenth)
+
+    def exchange(stage, chunk):
+        if stage == 0:
+            source, target = part.at[chunk, 1 - core], got_core.at[chunk]
+        elif stage == 1:
+            source, target = hold_x.at[chunk, 1 - x_half], got_x.at[chunk]
+        elif stage == 2:
+            source, target = hold_y.at[chunk, 1 - y_half], got_y.at[chunk]
+        elif stage == 3:
+            source, target = hold_a.at[chunk, 1 - a_half], got_a.at[chunk]
+        elif stage == 4:
+            source, target = hold_b.at[chunk, 1 - b_half], got_b.at[chunk]
+        else:
+            at, size = ((at_b, sixteenth), (at_a, eighth), (at_y, quarter))[stage - 5]
+            source = whole.at[chunk, pl.ds(at, size), :]
+            target = source
+        return pltpu.make_async_remote_copy(
+            src_ref=source,
+            dst_ref=target,
+            send_sem=send_sem.at[stage, chunk],
+            recv_sem=recv_sem.at[stage, chunk],
+            device_id=route[(0, 1, 2, 3, 4, 4, 3, 2)[stage]],
+            device_id_type=MESH,
+        )
+
+    def out_copy(chunk):
+        return pltpu.make_async_copy(whole.at[chunk], merged.at[chunk], out_sem.at[chunk])
+
+    def produce(chunk):
+        for copy in loads(chunk):
+            copy.wait()
+        slot = lax.rem(chunk, 2)
+        live = lax.broadcasted_iota(jnp.int32, (packed, width), 0) < total
+        left = jnp.where(live, left_in[slot], LOW(0))
+        right = jnp.where(live, right_in[slot], LOW(0))
+        product = dot(left, right, 0, 0).astype(LOW)
+        for shard in range(owners):
+            part[chunk, shard % 2, shard // 2] = product[shard * part_rows : (shard + 1) * part_rows]
+        exchange(0, chunk).start()
+
+    def add(mine, theirs):
+        return (mine.astype(F32) + theirs.astype(F32)).astype(LOW)
+
+    def take(stage, chunk):
+        exchange(stage - 1, chunk).wait_recv()
+        if stage == 1:
+            hold_x[chunk] = add(part[chunk, core], got_core[chunk])
+        elif stage == 2:
+            hold_y[chunk] = add(hold_x[chunk, x_half], got_x[chunk]).reshape(hold_y.shape[1:])
+        elif stage == 3:
+            hold_a[chunk] = add(hold_y[chunk, y_half], got_y[chunk]).reshape(hold_a.shape[1:])
+        elif stage == 4:
+            hold_b[chunk] = add(hold_a[chunk, a_half], got_a[chunk]).reshape(hold_b.shape[1:])
+        elif stage == 5:
+            whole[chunk, pl.ds(at_b, sixteenth), :] = add(hold_b[chunk, b_half], got_b[chunk])
+        if stage < 8:
+            exchange(stage, chunk).start()
+        else:
+            out_copy(chunk).start()
+
+    def sums_exchange(turn):
+        return pltpu.make_async_remote_copy(
+            src_ref=sums_hold.at[turn],
+            dst_ref=sums_got.at[turn],
+            send_sem=sums_send.at[turn],
+            recv_sem=sums_recv.at[turn],
+            device_id=route[turn],
+            device_id_type=MESH,
+        )
+
+    def back_copies():
+        sent = []
+        for which, (source, target) in enumerate(((grad, grad_back), (layer_out, layer_back))):
+            for place, other in enumerate(others):
+                sent.append(
+                    pltpu.make_async_remote_copy(
+                        src_ref=source.at[:, pl.ds(pl.multiple_of(other * rows, rows), rows), :],
+                        dst_ref=target.at[pl.ds(var * each, each)],
+                        send_sem=back_send.at[which, place],
+                        recv_sem=back_recv.at[which, place],
+                        device_id=(win, other),
+                        device_id_type=MESH,
+                    )
+                )
+        return sent
+
+    def own_copies():
+        return [
+            pltpu.make_async_copy(
+                source.at[:, pl.ds(pl.multiple_of(var * rows, rows), rows), :],
+                target.at[pl.ds(var * each, each)],
+                own_sem.at[which],
+            )
+            for which, (source, target) in enumerate(((grad, grad_back), (layer_out, layer_back)))
+        ]
+
+    for copy in loads(0):
+        copy.start()
+    for copy in own_copies():
+        copy.start()
+    sums_hold[0] = sums[...]
+    sums_exchange(0).start()
+
+    def step(now, carry):
+        @pl.when(now + 1 < chunks)
+        def _():
+            for copy in loads(now + 1):
+                copy.start()
+
+        @pl.when(now < chunks)
+        def _():
+            produce(now)
+
+        for stage in range(1, 9):
+            lag = LAGS[stage]
+
+            @pl.when(jnp.logical_and(now >= lag, now < chunks + lag))
+            def _(stage=stage, lag=lag):
+                take(stage, now - lag)
+
+        for turn in range(5):
+
+            @pl.when(now == 2 * turn + 4)
+            def _(turn=turn):
+                sums_exchange(turn).wait_recv()
+                summed = sums_hold[turn] + sums_got[turn]
+                if turn < 4:
+                    sums_hold[turn + 1] = summed
+                    sums_exchange(turn + 1).start()
+                else:
+                    sums_out[...] = summed
+
+        @pl.when(now == chunks + 1)
+        def _():
+            for copy in back_copies():
+                copy.start()
+
+        return carry
+
+    lax.fori_loop(0, chunks + LAGS[8], step, 0)
+
+    def settle(chunk, carry):
+        for stage in range(8):
+            exchange(stage, chunk).wait_send()
+        out_copy(chunk).wait()
+        return carry
+
+    lax.fori_loop(0, chunks, settle, 0)
+    for turn in range(5):
+        sums_exchange(turn).wait_send()
+    for copy in own_copies():
+        copy.wait()
+    for copy in back_copies():
+        copy.wait()
+
+
+def finish_kernel(
+    meta, merged, sums, layer_back, grad_back,
+    layer_out, grad_inputs, qkv, bias_qv, attn, out_bias, in_, bias_in, out, gain, shift,
+):
+    wins = layer_back.shape[0]
+    layers, width = qkv.shape[0], merged.shape[2]
+    part_rows = merged.shape[1]
+    per_layer = merged.shape[0] // layers
+    var = meta[meta.shape[0] - 2]
+    for place in range(wins):
+        window = meta[place]
+        layer_out[window] = layer_back[place]
+        grad_inputs[window] = grad_back[place].astype(F32)
+    narrow = out_bias.shape[2]
+    at = pl.multiple_of(var * narrow, narrow)
+    wide = bias_qv.shape[1]
+    for layer in range(layers):
+        base = (layers - 1 - layer) * per_layer
+        for which in range(3):
+            qkv[layer, :, which * width : (which + 1) * width] = merged[base + which].astype(F32)
+        attn[layer] = merged[base + 3].astype(F32)
+        for which in range(4):
+            in_[layer, :, which * width : (which + 1) * width] = merged[base + 4 + which].astype(F32)
+            out[layer, which * part_rows : (which + 1) * part_rows, :] = merged[base + 8 + which].astype(F32)
+        half = width // wide
+        bias_qv[layer : layer + 1, :] = sums[
+            layer, pl.ds(var // half, 1), pl.ds(pl.multiple_of(lax.rem(var, half) * wide, wide), wide)
+        ]
+        bias_in[layer : layer + 1, :] = sums[layer, pl.ds(4 + var, 1), :]
+        out_bias[layer] = sums[layer, 2:4, pl.ds(at, narrow)]
+        gain[layer] = sums[layer, 8:10, pl.ds(at, narrow)]
+        shift[layer] = sums[layer, 10:12, pl.ds(at, narrow)]
+
+
+def in_vmem(count):
+    return [pl.BlockSpec(memory_space=pltpu.VMEM)] * count
+
+
+def anywhere(count):
+    return [pl.BlockSpec(memory_space=pl.ANY)] * count
+
+
+def in_smem():
+    return [pl.BlockSpec(memory_space=pltpu.SMEM)]
+
+
+def shaped(shape, kind=LOW):
+    return jax.ShapeDtypeStruct(shape, kind)
+
+
+def whole_windows(
+    inputs, counts, row_index, w_qkv, bias_qv, w_attn_out, out_bias, w_in, bias_in, w_ffn_out,
+    norm_gain, norm_bias, cotangent,
+):
+    wins, rows, width = inputs.shape
+    owners, groups = lax.axis_size("var"), lax.axis_size("win")
+    each, length = wins // owners, rows * owners
+    packed = each * length
+    layers, hidden_width = w_in.shape[0], w_in.shape[2]
+    dma = pltpu.SemaphoreType.DMA
+
+    def params(**more):
+        return pltpu.CompilerParams(vmem_limit_bytes=VMEM_BYTES, **more)
+
+    x, g, meta = pl.pallas_call(
+        functools.partial(spread_kernel, owners),
+        name="spread",
+        out_shape=[shaped((each, length, width))] * 2 + [shaped((wins + 2 * each + 2,), jnp.int32)],
+        in_specs=in_smem() + in_vmem(2),
+        out_specs=anywhere(2) + in_smem(),
+        scratch_shapes=[pltpu.VMEM((wins, rows, width), LOW)] * 2 + [dma((owners - 1,))] * 4 + [dma((2,))],
+        compiler_params=params(collective_id=0, has_side_effects=True),
+    )(counts, inputs, cotangent)
+
+    weights = (w_qkv, w_attn_out, w_in, w_ffn_out)
+    weight_space = [pltpu.VMEM(weight.shape, LOW) for weight in weights]
+    kept = [
+        shaped((layers, packed, 3 * width)),
+        shaped((layers, packed, hidden_width)),
+        shaped((layers, 2, packed, width), F32),
+        shaped((layers, packed, 128), F32),
+        shaped((layers, packed, width), F32),
+    ]
+    kept_space = [pltpu.VMEM(entry.shape, entry.dtype) for entry in kept]
+    lefts_shape = shaped((layers, 7, packed, width))
+    lefts, *stash, layer_rows = pl.pallas_call(
+        forward_kernel,
+        name="forward",
+        out_shape=[lefts_shape] + kept + [shaped((each, length, width))],
+        in_specs=in_smem() + in_vmem(2) + anywhere(4) + in_vmem(5),
+        out_specs=anywhere(6) + in_vmem(1),
+        scratch_shapes=weight_space
+        + [pltpu.VMEM(lefts_shape.shape, LOW)]
+        + kept_space
+        + [pltpu.VMEM((packed, width), F32), dma((layers, 4)), dma((layers, 6, 2))],
+        compiler_params=params(),
+    )(meta, row_index, x, *weights, bias_qv, out_bias, bias_in, norm_gain, norm_bias)
+
+    rights_shape = shaped((layers, 9, packed, width))
+    rights, grad_rows, sums = pl.pallas_call(
+        backward_kernel,
+        name="backward",
+        out_shape=[rights_shape, shaped((each, length, width)), shaped((layers, 16, width), F32)],
+        in_specs=in_smem() + in_vmem(2) + anywhere(4) + in_vmem(1) + anywhere(5),
+        out_specs=anywhere(1) + in_vmem(2),
+        scratch_shapes=weight_space
+        + [pltpu.VMEM(rights_shape.shape, LOW)]
+        + kept_space
+        + [
+            pltpu.VMEM((packed, width), F32),
+            pltpu.VMEM((packed, width), LOW),
+            dma((layers, 4)),
+            dma((layers, 5, 2)),
+            dma((layers, 2)),
+        ],
+        compiler_params=params(),
+    )(meta, row_index, g, *weights, norm_gain, *stash)
+
+    chunks = layers * 12
+    part_rows = width // owners
+    half, quarter, eighth = part_rows // 2, part_rows // 4, part_rows // 8
+
+    def space(*shape):
+        return pltpu.VMEM((chunks,) + shape + (width,), LOW)
+
+    merged, sums, layer_back, grad_back = pl.pallas_call(
+        functools.partial(merge_kernel, owners),
+        name="merge",
+        out_shape=[
+            shaped((chunks, part_rows, width)),
+            shaped(sums.shape, F32),
+            shaped((wins, rows, width)),
+            shaped((wins, rows, width)),
+        ],
+        in_specs=in_smem() + anywhere(2) + in_vmem(3),
+        out_specs=anywhere(1) + in_vmem(1) + anywhere(2),
+        scratch_shapes=[pltpu.VMEM((2, packed, width), LOW)] * 2
+        + [
+            space(2, 2, part_rows),
+            space(2, part_rows),
+            space(2, part_rows),
+            space(part_rows),
+            space(2, half),
+            space(half),
+            space(2, quarter),
+            space(quarter),
+            space(2, eighth),
+            space(eighth),
+            space(part_rows),
+        ]
+        + [pltpu.VMEM((5,) + sums.shape, F32)] * 2
+        + [dma((2, 2)), dma((8, chunks)), dma((8, chunks)), dma((chunks,))]
+        + [dma((5,))] * 2
+        + [dma((2, owners - 1))] * 2
+        + [dma((2,))],
+        compiler_params=params(collective_id=1, has_side_effects=True),
+    )(meta, lefts, rights, sums, layer_rows, grad_rows)
+
+    narrow = width // owners
+    return pl.pallas_call(
+        finish_kernel,
+        name="finish",
+        out_shape=[
+            shaped((wins, rows, width)),
+            shaped((wins, rows, width), F32),
+            shaped((layers, narrow, 3 * width), F32),
+            shaped((layers, 2 * narrow), F32),
+            shaped((layers, narrow, width), F32),
+            shaped((layers, 2, narrow), F32),
+            shaped((layers, narrow, hidden_width), F32),
+            shaped((layers, hidden_width // owners), F32),
+            shaped((layers, hidden_width // owners, width), F32),
+            shaped((layers, 2, narrow), F32),
+            shaped((layers, 2, narrow), F32),
+        ],
+        in_specs=in_smem() + in_vmem(4),
+        out_specs=in_vmem(11),
+        compiler_params=params(),
+    )(meta, merged, sums, layer_back, grad_back)
+
+
+def choose(*arrays):
+    wins, rows, width = arrays[0].shape
+    owners, groups = lax.axis_size("var"), lax.axis_size("win")
+    fits = owners == 4 and groups == 8 and wins % owners == 0 and rows % 16 == 0
+    fits = fits and (wins // owners, rows * owners, width, arrays[7].shape[2]) == (3, 256, 512, 2048)
+    return whole_windows(*arrays) if fits else per_device(*arrays)
+
+
 def solution(mesh):
     return jax.shard_map(
-        per_device,
+        choose,
         mesh=mesh,
         in_specs=(
             P("win", "var", None),

time: 861 us -> 195 us (0.23)
  waiting for transfers between devices: 497 us -> 0 us
  Pallas kernels: 0 us -> 195 us
  local copies, waits for them, and re-layouts: 121 us -> 0 us
  matrix products: 120 us -> 0 us
  other arithmetic: 75.5 us -> 0 us
  blocking collectives: 22.2 us -> 0 us
  between operations: 15.6 us -> 0.68 us
    reduce_scatter x5 -> x0, waiting for transfers between devices: 214 us -> none  [the longest x2 96.1 us: per_device(): lax.psum_scatter(jnp.concatenate([d_key.reshape(span_rows, wins, width),...]
    pallas_call x0 -> x5, Pallas kernels: none -> 195 us  [the longest x1 109 us: whole_windows(): pl.pallas_call(functools.partial(merge_kernel, owners), name='merge', out...]
    dot_general x36 -> x0, matrix products: 120 us -> none  [the longest x2 13.8 us: per_device(): jnp.einsum('rd,fd->rf', d_ffn, w_ffn_out[which_layer], preferred_element_...]
    psum x1 -> x0, waiting for transfers between devices: 110 us -> none  [per_device(): lax.psum(shards[0].astype(jnp.bfloat16), 'win').astype(jnp.float32)]
    unnamed x20 -> x0, waiting for transfers between devices: 106 us -> none
    all_gather x2 -> x0, waiting for transfers between devices: 68 us -> none  [per_device(): whole = lax.all_gather(pair, 'var', axis=1, tiled=True)]
    unnamed x186 -> x0, local copies, waits for them, and re-layouts: 47 us -> none
    reshape x20 -> x0, local copies, waits for them, and re-layouts: 30.7 us -> none  [the longest x4 9.53 us: per_device(): grad_heads = d_mixed.reshape(wins, rows, head_count, head_size)]
  transfers between devices with their start and end apart: 14 -> 0, of which waited for: 14 -> 0; matrix products, arithmetic and copies ran while one was open for 11% -> 0% of each run, Pallas kernels for 0% -> 0%
where the time goes in v1:
time: 195 us
  Pallas kernels  195 us (100%)
    pallas_call x1, Pallas kernels, whole_windows(): pl.pallas_call(functools.partial(merge_kernel, owners), name='merge', out...  109 us
    pallas_call x1, Pallas kernels, whole_windows(): pl.pallas_call(forward_kernel, name='forward', out_shape=[lefts_shape] +...  28.9 us
    pallas_call x1, Pallas kernels, whole_windows(): pl.pallas_call(backward_kernel, name='backward', out_shape=[rights_shape,...  28 us
    pallas_call x1, Pallas kernels, whole_windows(): pl.pallas_call(functools.partial(spread_kernel, owners), name='spread', o...  22.6 us
    pallas_call x1, Pallas kernels, whole_windows(): pl.pallas_call(finish_kernel, name='finish', out_shape=[shaped((wins, row...  5.96 us

profile of v1, /device:TPU:0, one launch (start us, length us, event | category | flops | bytes accessed | tf_op | source)
XLA Modules:
  0.0 195.2 jit_solution(12851665037052114433)
XLA Ops:
  0.6 22.6 %spread.1 = (bf16[3,256,512]{2,1,0:T(8,128)(2,1)}, bf16[3,256,512]{2,1,0:T(8,128)(2,1)}, s32[20]{0:T(128)}) custom-call(s32[12]{0:T(128)} %counts.1, bf16[12,64,512]{2,1,0:T(8,128)(2,1)} %x.1, bf16[12,64,512]{2,1,0:T(8,128)(2,1)} %g.1), custom_call_target="tpu_custom_call" | custom-call | tf_op jit(solution)/shard_map/spread/pallas_call | solution.py:1081
  23.2 28.9 %forward.1 = (bf16[2,7,768,512]{3,2,1,0:T(8,128)(2,1)}, bf16[2,768,1536]{2,1,0:T(8,128)(2,1)}, bf16[2,768,2048]{2,1,0:T(8,128)(2,1)}, f32[2,2,768,512]{3,2,1,0:T...) custom-call(s32[20]{0:T(128)} %get-tuple-element.28.meta, ...), custom_call_target="tpu_custom_call" | custom-call | tf_op jit(solution)/shard_map/forward/pallas_call | solution.py:1102
  52.1 28.0 %backward.1 = (bf16[2,9,768,512]{3,2,1,0:T(8,128)(2,1)}, bf16[3,256,512]{2,1,0:T(8,128)(2,1)}, f32[2,16,512]{2,1,0:T(8,128)}) custom-call(s32[20]{0:T(128)} %get-tuple-element.28.meta, s32[12,256]{1,0:T(8,128)} %row_index.3, bf16[3,256,512]{2,1,0:T(8,128)(2,1)} %get-tuple-element.31.g, bf16[2,512,1536]{2,1,0:T(8,128)(2,1)} %w_qkv.3, ...), custom_call_target="tpu_custom_call" | custom-call | tf_op jit(solution)/shard_map/backward/pallas_call | solution.py:1116
  80.2 109.1 %merge.1 = (bf16[24,128,512]{2,1,0:T(8,128)(2,1)}, f32[2,16,512]{2,1,0:T(8,128)}, bf16[12,64,512]{2,1,0:T(8,128)(2,1)}, bf16[12,64,512]{2,1,0:T(8,128)(2,1)}) custom-call(s32[20]{0:T(128)} %get-tuple-element.28.meta, bf16[2,7,768,512]{3,2,1,0:T(8,128)(2,1)} %get-tuple-element.30.lefts, bf16[2,9,768,512]{3,2,1,0:T(8,128)(2,1)} %get-tuple-element.37.rights, ...), custom_call_target="tpu_custom_call" | custom-call | tf_op jit(solution)/shard_map/merge/pallas_call | solution.py:1142
  189.2 6.0 %finish.1 = (bf16[12,64,512]{2,1,0:T(8,128)(2,1)}, f32[12,64,512]{2,1,0:T(8,128)}, f32[2,128,1536]{2,1,0:T(8,128)}, f32[2,256]{1,0:T(2,128)}, f32[2,128,512]{2,1...) custom-call(s32[20]{0:T(128)} %get-tuple-element.28.meta, ...), custom_call_target="tpu_custom_call" | custom-call | tf_op jit(solution)/shard_map/finish/pallas_call | solution.py:1176
